TPU v7x, 32 devices: a whole 2x2x4 slice. The times are simulated.
32 devices in a mesh: dp: 8 (over z, core), mp: 4 (over y, x).
Axes of the slice: x: 2, y: 2, z: 4, core: 2. Of those that a mesh axis runs over, the one named last changes fastest.
Arguments:
- picture_summary_vectors: bfloat16 [4096, 1152], P(('dp', 'mp')), may hold values from -6 to 6
- caption_summary_vectors: bfloat16 [4096, 1152], P(('dp', 'mp')), may hold values from -6 to 6
- picture_mapping_matrix: bfloat16 [1152, 1152], P(('dp', 'mp')), may hold values from -0.1875 to 0.1875
- caption_mapping_matrix: bfloat16 [1152, 1152], P(('dp', 'mp')), may hold values from -0.1875 to 0.1875
- picture_partner_label: int32 [4096], P(('dp', 'mp')), may hold values from 0 to 1023
- caption_partner_label: int32 [4096], P(('dp', 'mp')), may hold values from 0 to 1023
- similarity_factor: float32 [1], replicated, may hold values from 5 to 15
- offset_term: float32 [1], replicated, may hold values from -4 to -1
Outputs:
- img_grad: bfloat16 [4096, 1152], P(('dp', 'mp'))
- txt_grad: bfloat16 [4096, 1152], P(('dp', 'mp'))
- w_img_grad: float32 [1152, 1152], P(('dp', 'mp'))
- w_txt_grad: float32 [1152, 1152], P(('dp', 'mp'))
All inputs are finite; a program needn't handle non-finite values.
Results may differ from a plain program's by a relative error of at most 0.023.
Values may be sent and summed in bfloat16 or wider, within the bound.
A program may use at most 128 MiB of HBM per device.

v0:
```python
import jax
import jax.numpy as jnp
from jax import lax
from jax.sharding import PartitionSpec as P


def passed_along(value, axis, steps):
    count = lax.axis_size(axis)
    pairs = [(source, (source + steps) % count) for source in range(count)]
    return lax.ppermute(value, axis, pairs)


def embed(feat, weight):
    pre = jnp.dot(feat, weight, preferred_element_type=jnp.float32)
    radius = jnp.sqrt(jnp.sum(pre * pre, axis=1, keepdims=True) + 1e-06)
    return (pre / radius, radius)


def pair_terms(big_emb, big_ids, text_emb, text_ids, similarity_multiplier, offset):
    logits = (
        similarity_multiplier
        * lax.dot_general(
            big_emb, text_emb, (((1,), (1,)), ((), ())), preferred_element_type=jnp.float32
        )
        + offset
    )
    sign = jnp.where(big_ids[:, None] == text_ids[None, :], 1.0, -1.0).astype(jnp.float32)
    slope = (-sign * jax.nn.sigmoid(-sign * logits)).astype(jnp.bfloat16)
    image_part = jnp.dot(slope, text_emb, preferred_element_type=jnp.float32)
    text_part = lax.dot_general(
        slope, big_emb, (((0,), (0,)), ((), ())), preferred_element_type=jnp.float32
    )
    return (image_part, text_part)


def backward_rows(unit, radius, grad, feat, weight):
    d_pre = ((grad - unit * jnp.sum(unit * grad, axis=1, keepdims=True)) / radius).astype(
        jnp.bfloat16
    )
    d_feat = lax.dot_general(
        d_pre, weight, (((1,), (1,)), ((), ())), preferred_element_type=jnp.float32
    ).astype(jnp.bfloat16)
    d_weight = lax.dot_general(
        feat, d_pre, (((0,), (0,)), ((), ())), preferred_element_type=jnp.float32
    )
    return (d_feat, d_weight)


def on_device(
    picture_summary_vectors,
    caption_summary_vectors,
    picture_mapping_matrix,
    caption_mapping_matrix,
    picture_partner_label,
    caption_partner_label,
    similarity_factor,
    offset_term,
):
    full_img, full_txt = (
        lax.all_gather(picture_mapping_matrix, ("dp", "mp"), axis=0, tiled=True),
        lax.all_gather(caption_mapping_matrix, ("dp", "mp"), axis=0, tiled=True),
    )
    unit_img, rad_img = embed(picture_summary_vectors, full_img)
    unit_txt, rad_txt = embed(caption_summary_vectors, full_txt)
    emb_img = unit_img.astype(jnp.bfloat16)
    emb_txt = unit_txt.astype(jnp.bfloat16)
    big_emb, big_ids = (
        lax.all_gather(emb_img, "mp", axis=0, tiled=True),
        lax.all_gather(picture_partner_label, "mp", axis=0, tiled=True),
    )
    similarity_multiplier = similarity_factor[0]
    offset = offset_term[0]
    rows = emb_txt.shape[0]
    width = emb_txt.shape[1]
    turns = lax.axis_size("dp")
    image_sum = jnp.zeros((big_emb.shape[0], width), jnp.float32)

    def turn(step, carry):
        image_total, text_emb, text_ids, text_total = carry
        image_part, text_part = pair_terms(
            big_emb, big_ids, text_emb, text_ids, similarity_multiplier, offset
        )
        image_total = image_total + image_part
        text_total = text_total + text_part
        text_emb, text_ids = passed_along((text_emb, text_ids), "dp", 1)
        text_total = passed_along(text_total, "dp", 1)
        return (image_total, text_emb, text_ids, text_total)

    start = (image_sum, emb_txt, caption_partner_label, jnp.zeros((rows, width), jnp.float32))
    image_sum, moved_emb, moved_ids, text_sum = lax.fori_loop(0, turns, turn, start)
    d_emb_txt = similarity_multiplier * text_sum
    d_emb_img = similarity_multiplier * lax.psum_scatter(
        image_sum.astype(jnp.bfloat16), "mp", scatter_dimension=0, tiled=True
    ).astype(jnp.float32)
    img_grad, d_w_img = backward_rows(
        unit_img, rad_img, d_emb_img, picture_summary_vectors, full_img
    )
    txt_grad, d_w_txt = backward_rows(
        unit_txt, rad_txt, d_emb_txt, caption_summary_vectors, full_txt
    )
    w_img_grad, w_txt_grad = (
        lax.psum_scatter(d_w_img, ("dp", "mp"), scatter_dimension=0, tiled=True),
        lax.psum_scatter(d_w_txt, ("dp", "mp"), scatter_dimension=0, tiled=True),
    )
    return (img_grad, txt_grad, w_img_grad, w_txt_grad)


def solution(mesh):
    in_specs = (
        P(("dp", "mp"), None),
        P(("dp", "mp"), None),
        P(("dp", "mp"), None),
        P(("dp", "mp"), None),
        P(("dp", "mp")),
        P(("dp", "mp")),
        P(),
        P(),
    )
    out_specs = (
        P(("dp", "mp"), None),
        P(("dp", "mp"), None),
        P(("dp", "mp"), None),
        P(("dp", "mp"), None),
    )
    return jax.shard_map(
        on_device, mesh=mesh, in_specs=in_specs, out_specs=out_specs, check_vma=False
    )
```

profile of v0, /device:TPU:0, one launch (start us, length us, event | category | flops | bytes accessed | tf_op | source)
XLA Modules:
  0.0 584.3 jit_solution(3399188849460991183)
XLA Ops:
  8.7 63.8 %all-gather.11.cloned.1.call-done = bf16[32,36,1152]{2,1,0:T(8,128)(2,1)} async-done(((bf16[1,36,1152]{2,1,0:T(8,128)(2,1)}), bf16[32,36,1152]{2,1,0:T(8,128)(2,1)}) %all-gather.11.cloned.1.call-update) | async-done | bytes 2654224 | tf_op jit(solution)/shard_map/all_gather | solution.py:60
  72.5 3.6 reshape.29
  78.7 7.9 %all-gather.1 = s32[4,1,128]{2,1,0:T(1,128)S(1)} all-gather(s32[1,1,128]{2,1,0:T(1,128)S(1)} %bitcast.49), channel_id=1, replica_groups=mesh['dp'=8,'mp'=4] {'mp'}, dimensions={0}, use_global_device_ids=true | all-gather | bytes 2560 | tf_op jit(solution)/shard_map/all_gather | solution.py:69
  86.6 46.4 %all-gather.9.cloned.1.call-done = bf16[32,36,1152]{2,1,0:T(8,128)(2,1)} async-done(((bf16[1,36,1152]{2,1,0:T(8,128)(2,1)}), bf16[32,36,1152]{2,1,0:T(8,128)(2,1)}) %all-gather.9.cloned.1.call-update) | async-done | bytes 2654224 | tf_op jit(solution)/shard_map/all_gather | solution.py:61
  133.1 5.2 reshape.25
  138.2 2.4 multiply_reduce_fusion.3
  142.4 19.6 %all-gather.7.cloned.1.call-done = bf16[512,1152]{1,0:T(8,128)(2,1)} async-done(((bf16[128,1152]{1,0:T(8,128)(2,1)}), bf16[512,1152]{1,0:T(8,128)(2,1)}) %all-gather.7.cloned.1.call-update) | async-done | bytes 1179664 | tf_op jit(solution)/shard_map/all_gather | solution.py:68
  162.0 163.8 %while.17 = (s32[]{:T(128)}, f32[512,1152]{1,0:T(8,128)S(1)}, bf16[128,1152]{1,0:T(8,128)(2,1)}, s32[128]{0:T(128)S(1)}, f32[128,1152]{1,0:T(8,128)S(1)}, /*inde...) while((s32[]{:T(128)}, f32[512,1152]{1,0:T(8,128)S(1)}, ...), condition=%wide.region_3.4_spmd.clone, body=%wide.region_2.3_spmd.clone.sunk | while | flops 455032832 | bytes 18618160 | solution.py:90
  163.6 3.1 fusion.37
  171.2 11.3 %collective-permute-done.1 = s32[128]{0:T(128)S(1)} collective-permute-done((s32[128]{0:T(128)}, s32[128]{0:T(128)S(1)}, u32[]{:S(2)}, u32[]{:S(2)}) %collective-permute-start.1) | collective-permute-done | bytes 544 | tf_op jit(solution)/shard_map/while/body/eval_jaxpr/ppermute | solution.py:10
  184.1 3.1 fusion.37
  190.1 12.9 %collective-permute-done.1 = s32[128]{0:T(128)S(1)} collective-permute-done((s32[128]{0:T(128)}, s32[128]{0:T(128)S(1)}, u32[]{:S(2)}, u32[]{:S(2)}) %collective-permute-start.1) | collective-permute-done | bytes 544 | tf_op jit(solution)/shard_map/while/body/eval_jaxpr/ppermute | solution.py:10
  204.6 3.1 fusion.37
  210.6 12.9 %collective-permute-done.1 = s32[128]{0:T(128)S(1)} collective-permute-done((s32[128]{0:T(128)}, s32[128]{0:T(128)S(1)}, u32[]{:S(2)}, u32[]{:S(2)}) %collective-permute-start.1) | collective-permute-done | bytes 544 | tf_op jit(solution)/shard_map/while/body/eval_jaxpr/ppermute | solution.py:10
  225.1 3.1 fusion.37
  231.1 12.9 %collective-permute-done.1 = s32[128]{0:T(128)S(1)} collective-permute-done((s32[128]{0:T(128)}, s32[128]{0:T(128)S(1)}, u32[]{:S(2)}, u32[]{:S(2)}) %collective-permute-start.1) | collective-permute-done | bytes 544 | tf_op jit(solution)/shard_map/while/body/eval_jaxpr/ppermute | solution.py:10
  245.5 3.1 fusion.37
  251.6 12.9 %collective-permute-done.1 = s32[128]{0:T(128)S(1)} collective-permute-done((s32[128]{0:T(128)}, s32[128]{0:T(128)S(1)}, u32[]{:S(2)}, u32[]{:S(2)}) %collective-permute-start.1) | collective-permute-done | bytes 544 | tf_op jit(solution)/shard_map/while/body/eval_jaxpr/ppermute | solution.py:10
  266.0 3.1 fusion.37
  272.0 12.9 %collective-permute-done.1 = s32[128]{0:T(128)S(1)} collective-permute-done((s32[128]{0:T(128)}, s32[128]{0:T(128)S(1)}, u32[]{:S(2)}, u32[]{:S(2)}) %collective-permute-start.1) | collective-permute-done | bytes 544 | tf_op jit(solution)/shard_map/while/body/eval_jaxpr/ppermute | solution.py:10
  286.5 3.1 fusion.37
  292.5 12.9 %collective-permute-done.1 = s32[128]{0:T(128)S(1)} collective-permute-done((s32[128]{0:T(128)}, s32[128]{0:T(128)S(1)}, u32[]{:S(2)}, u32[]{:S(2)}) %collective-permute-start.1) | collective-permute-done | bytes 544 | tf_op jit(solution)/shard_map/while/body/eval_jaxpr/ppermute | solution.py:10
  307.0 3.1 fusion.37
  313.0 12.9 %collective-permute-done.1 = s32[128]{0:T(128)S(1)} collective-permute-done((s32[128]{0:T(128)}, s32[128]{0:T(128)S(1)}, u32[]{:S(2)}, u32[]{:S(2)}) %collective-permute-start.1) | collective-permute-done | bytes 544 | tf_op jit(solution)/shard_map/while/body/eval_jaxpr/ppermute | solution.py:10
  329.1 3.3 convolution_bitcast_fusion
  332.4 20.5 %reduce-scatter.4.cloned.1.call-done = bf16[128,1152]{1,0:T(8,128)(2,1)} async-done(((bf16[512,1152]{1,0:T(8,128)(2,1)}), bf16[128,1152]{1,0:T(8,128)(2,1)}) %reduce-scatter.4.cloned.1.call-update) | async-done | bytes 294928 | tf_op jit(solution)/shard_map/reduce_scatter | solution.py:92
  354.2 4.2 convolution_bitcast_fusion.1
  358.5 1.7 copy-done.5
  360.2 2.9 convolution_convert_fusion
  363.0 1.7 convolution_convert_fusion.1
  364.7 209.2 %all-reduce.5.cloned.1.call-done = (f32[1152,1152]{0,1:T(8,128)}, f32[1152,1152]{0,1:T(8,128)}) async-done(((f32[1152,1152]{0,1:T(8,128)}, f32[1152,1152]{0,1:T(8,128)}), (f32[1152,1152]{0,1:T(8,128)}, f32[1152,1152]{0,1:T(8,128)})) %all-reduce.5.cloned.1.call-update) | async-done | bytes 10616848
  573.9 2.0 constant_dynamic-slice_fusion
  (153 shorter events, 48.6 us)
Async XLA Ops:
  7.2 131.1 %copy-start = (bf16[128,1152]{1,0:T(8,128)(2,1)S(1)}, bf16[128,1152]{1,0:T(8,128)(2,1)}, u32[]{:S(2)}) copy-start(bf16[128,1152]{1,0:T(8,128)(2,1)} %param.11) | copy-start | bytes 884740
  7.2 65.3 %all-gather.11.cloned.1.call-start = ((), (), s32[]{:S(2)}) async-start(), calls=%async_computation.4 | async-start | bytes 3041280 | tf_op jit(solution)/shard_map/all_gather | solution.py:60
  7.9 125.1 %all-gather.9.cloned.1.call-start = ((), (), s32[]{:S(2)}) async-start(), calls=%async_computation.3 | async-start | bytes 3041280 | tf_op jit(solution)/shard_map/all_gather | solution.py:61
  8.7 67.4 %copy-start.11 = (bf16[128,1152]{1,0:T(8,128)(2,1)S(1)}, bf16[128,1152]{1,0:T(8,128)(2,1)}, u32[]{:S(2)}) copy-start(bf16[128,1152]{1,0:T(8,128)(2,1)} %param.10) | copy-start | bytes 884740
  8.7 153.3 %all-gather.7.cloned.1.call-start = ((), (), s32[]{:S(2)}) async-start(), calls=%async_computation.1 | async-start | bytes 1474560 | tf_op jit(solution)/shard_map/all_gather | solution.py:68
  78.7 274.3 %reduce-scatter.4.cloned.1.call-start = ((), (), s32[]{:S(2)}) async-start(), calls=%async_computation.2 | async-start | bytes 1474560 | tf_op jit(solution)/shard_map/reduce_scatter | solution.py:92
  167.9 14.6 %collective-permute-start.2 = (f32[128,1152]{1,0:T(8,128)}, f32[128,1152]{1,0:T(8,128)S(1)}, u32[]{:S(2)}, u32[]{:S(2)}) collective-permute-start(f32[128,1152]{1,0:T(8,128)} %convolution_add_fusion.5), channel_id=1, source_target_pairs={{0,4},{4,8},{8,12},{12,16},{16,20},{20,24},{24,28},{28,0},{1,5},{5... | collective-permute-start | bytes 1769480 | tf_op jit(solution)/shard_map/while/body/eval_jaxpr/ppermute | solution.py:10
  167.9 14.6 %collective-permute-start = (bf16[128,1152]{1,0:T(8,128)(2,1)S(1)}, bf16[128,1152]{1,0:T(8,128)(2,1)}, u32[]{:S(2)}, u32[]{:S(2)}) collective-permute-start(bf16[128,1152]{1,0:T(8,128)(2,1)S(1)} %copy.29), channel_id=1, source_target_pairs={{0,4},{4,8},{8,12},{12,16},{16,20},{20,24},{24,28},{28,0},{1,5},{5... | collective-permute-start | bytes 884744 | tf_op jit(solution)/shard_map/while/body/eval_jaxpr/ppermute | solution.py:10
  169.5 13.0 %collective-permute-start.1 = (s32[128]{0:T(128)}, s32[128]{0:T(128)S(1)}, u32[]{:S(2)}, u32[]{:S(2)}) collective-permute-start(s32[128]{0:T(128)} %copy.30), channel_id=1, source_target_pairs={{0,4},{4,8},{8,12},{12,16},{16,20},{20,24},{24,28},{28,0},{1,5},{5... | collective-permute-start | bytes 1544 | tf_op jit(solution)/shard_map/while/body/eval_jaxpr/ppermute | solution.py:10
  188.4 14.6 %collective-permute-start.2 = (f32[128,1152]{1,0:T(8,128)}, f32[128,1152]{1,0:T(8,128)S(1)}, u32[]{:S(2)}, u32[]{:S(2)}) collective-permute-start(f32[128,1152]{1,0:T(8,128)} %convolution_add_fusion.5), channel_id=1, source_target_pairs={{0,4},{4,8},{8,12},{12,16},{16,20},{20,24},{24,28},{28,0},{1,5},{5... | collective-permute-start | bytes 1769480 | tf_op jit(solution)/shard_map/while/body/eval_jaxpr/ppermute | solution.py:10
  188.4 14.6 %collective-permute-start = (bf16[128,1152]{1,0:T(8,128)(2,1)S(1)}, bf16[128,1152]{1,0:T(8,128)(2,1)}, u32[]{:S(2)}, u32[]{:S(2)}) collective-permute-start(bf16[128,1152]{1,0:T(8,128)(2,1)S(1)} %copy.29), channel_id=1, source_target_pairs={{0,4},{4,8},{8,12},{12,16},{16,20},{20,24},{24,28},{28,0},{1,5},{5... | collective-permute-start | bytes 884744 | tf_op jit(solution)/shard_map/while/body/eval_jaxpr/ppermute | solution.py:10
  188.4 14.6 %collective-permute-start.1 = (s32[128]{0:T(128)}, s32[128]{0:T(128)S(1)}, u32[]{:S(2)}, u32[]{:S(2)}) collective-permute-start(s32[128]{0:T(128)} %copy.30), channel_id=1, source_target_pairs={{0,4},{4,8},{8,12},{12,16},{16,20},{20,24},{24,28},{28,0},{1,5},{5... | collective-permute-start | bytes 1544 | tf_op jit(solution)/shard_map/while/body/eval_jaxpr/ppermute | solution.py:10
  208.9 14.6 %collective-permute-start.2 = (f32[128,1152]{1,0:T(8,128)}, f32[128,1152]{1,0:T(8,128)S(1)}, u32[]{:S(2)}, u32[]{:S(2)}) collective-permute-start(f32[128,1152]{1,0:T(8,128)} %convolution_add_fusion.5), channel_id=1, source_target_pairs={{0,4},{4,8},{8,12},{12,16},{16,20},{20,24},{24,28},{28,0},{1,5},{5... | collective-permute-start | bytes 1769480 | tf_op jit(solution)/shard_map/while/body/eval_jaxpr/ppermute | solution.py:10
  208.9 14.6 %collective-permute-start = (bf16[128,1152]{1,0:T(8,128)(2,1)S(1)}, bf16[128,1152]{1,0:T(8,128)(2,1)}, u32[]{:S(2)}, u32[]{:S(2)}) collective-permute-start(bf16[128,1152]{1,0:T(8,128)(2,1)S(1)} %copy.29), channel_id=1, source_target_pairs={{0,4},{4,8},{8,12},{12,16},{16,20},{20,24},{24,28},{28,0},{1,5},{5... | collective-permute-start | bytes 884744 | tf_op jit(solution)/shard_map/while/body/eval_jaxpr/ppermute | solution.py:10
  208.9 14.6 %collective-permute-start.1 = (s32[128]{0:T(128)}, s32[128]{0:T(128)S(1)}, u32[]{:S(2)}, u32[]{:S(2)}) collective-permute-start(s32[128]{0:T(128)} %copy.30), channel_id=1, source_target_pairs={{0,4},{4,8},{8,12},{12,16},{16,20},{20,24},{24,28},{28,0},{1,5},{5... | collective-permute-start | bytes 1544 | tf_op jit(solution)/shard_map/while/body/eval_jaxpr/ppermute | solution.py:10
  229.4 14.6 %collective-permute-start.2 = (f32[128,1152]{1,0:T(8,128)}, f32[128,1152]{1,0:T(8,128)S(1)}, u32[]{:S(2)}, u32[]{:S(2)}) collective-permute-start(f32[128,1152]{1,0:T(8,128)} %convolution_add_fusion.5), channel_id=1, source_target_pairs={{0,4},{4,8},{8,12},{12,16},{16,20},{20,24},{24,28},{28,0},{1,5},{5... | collective-permute-start | bytes 1769480 | tf_op jit(solution)/shard_map/while/body/eval_jaxpr/ppermute | solution.py:10
  229.4 14.6 %collective-permute-start = (bf16[128,1152]{1,0:T(8,128)(2,1)S(1)}, bf16[128,1152]{1,0:T(8,128)(2,1)}, u32[]{:S(2)}, u32[]{:S(2)}) collective-permute-start(bf16[128,1152]{1,0:T(8,128)(2,1)S(1)} %copy.29), channel_id=1, source_target_pairs={{0,4},{4,8},{8,12},{12,16},{16,20},{20,24},{24,28},{28,0},{1,5},{5... | collective-permute-start | bytes 884744 | tf_op jit(solution)/shard_map/while/body/eval_jaxpr/ppermute | solution.py:10
  229.4 14.6 %collective-permute-start.1 = (s32[128]{0:T(128)}, s32[128]{0:T(128)S(1)}, u32[]{:S(2)}, u32[]{:S(2)}) collective-permute-start(s32[128]{0:T(128)} %copy.30), channel_id=1, source_target_pairs={{0,4},{4,8},{8,12},{12,16},{16,20},{20,24},{24,28},{28,0},{1,5},{5... | collective-permute-start | bytes 1544 | tf_op jit(solution)/shard_map/while/body/eval_jaxpr/ppermute | solution.py:10
  249.8 14.6 %collective-permute-start.2 = (f32[128,1152]{1,0:T(8,128)}, f32[128,1152]{1,0:T(8,128)S(1)}, u32[]{:S(2)}, u32[]{:S(2)}) collective-permute-start(f32[128,1152]{1,0:T(8,128)} %convolution_add_fusion.5), channel_id=1, source_target_pairs={{0,4},{4,8},{8,12},{12,16},{16,20},{20,24},{24,28},{28,0},{1,5},{5... | collective-permute-start | bytes 1769480 | tf_op jit(solution)/shard_map/while/body/eval_jaxpr/ppermute | solution.py:10
  249.8 14.6 %collective-permute-start = (bf16[128,1152]{1,0:T(8,128)(2,1)S(1)}, bf16[128,1152]{1,0:T(8,128)(2,1)}, u32[]{:S(2)}, u32[]{:S(2)}) collective-permute-start(bf16[128,1152]{1,0:T(8,128)(2,1)S(1)} %copy.29), channel_id=1, source_target_pairs={{0,4},{4,8},{8,12},{12,16},{16,20},{20,24},{24,28},{28,0},{1,5},{5... | collective-permute-start | bytes 884744 | tf_op jit(solution)/shard_map/while/body/eval_jaxpr/ppermute | solution.py:10
  249.9 14.6 %collective-permute-start.1 = (s32[128]{0:T(128)}, s32[128]{0:T(128)S(1)}, u32[]{:S(2)}, u32[]{:S(2)}) collective-permute-start(s32[128]{0:T(128)} %copy.30), channel_id=1, source_target_pairs={{0,4},{4,8},{8,12},{12,16},{16,20},{20,24},{24,28},{28,0},{1,5},{5... | collective-permute-start | bytes 1544 | tf_op jit(solution)/shard_map/while/body/eval_jaxpr/ppermute | solution.py:10
  270.3 14.6 %collective-permute-start.2 = (f32[128,1152]{1,0:T(8,128)}, f32[128,1152]{1,0:T(8,128)S(1)}, u32[]{:S(2)}, u32[]{:S(2)}) collective-permute-start(f32[128,1152]{1,0:T(8,128)} %convolution_add_fusion.5), channel_id=1, source_target_pairs={{0,4},{4,8},{8,12},{12,16},{16,20},{20,24},{24,28},{28,0},{1,5},{5... | collective-permute-start | bytes 1769480 | tf_op jit(solution)/shard_map/while/body/eval_jaxpr/ppermute | solution.py:10
  270.3 14.6 %collective-permute-start = (bf16[128,1152]{1,0:T(8,128)(2,1)S(1)}, bf16[128,1152]{1,0:T(8,128)(2,1)}, u32[]{:S(2)}, u32[]{:S(2)}) collective-permute-start(bf16[128,1152]{1,0:T(8,128)(2,1)S(1)} %copy.29), channel_id=1, source_target_pairs={{0,4},{4,8},{8,12},{12,16},{16,20},{20,24},{24,28},{28,0},{1,5},{5... | collective-permute-start | bytes 884744 | tf_op jit(solution)/shard_map/while/body/eval_jaxpr/ppermute | solution.py:10
  270.3 14.6 %collective-permute-start.1 = (s32[128]{0:T(128)}, s32[128]{0:T(128)S(1)}, u32[]{:S(2)}, u32[]{:S(2)}) collective-permute-start(s32[128]{0:T(128)} %copy.30), channel_id=1, source_target_pairs={{0,4},{4,8},{8,12},{12,16},{16,20},{20,24},{24,28},{28,0},{1,5},{5... | collective-permute-start | bytes 1544 | tf_op jit(solution)/shard_map/while/body/eval_jaxpr/ppermute | solution.py:10
  290.8 14.6 %collective-permute-start.2 = (f32[128,1152]{1,0:T(8,128)}, f32[128,1152]{1,0:T(8,128)S(1)}, u32[]{:S(2)}, u32[]{:S(2)}) collective-permute-start(f32[128,1152]{1,0:T(8,128)} %convolution_add_fusion.5), channel_id=1, source_target_pairs={{0,4},{4,8},{8,12},{12,16},{16,20},{20,24},{24,28},{28,0},{1,5},{5... | collective-permute-start | bytes 1769480 | tf_op jit(solution)/shard_map/while/body/eval_jaxpr/ppermute | solution.py:10
  290.8 14.6 %collective-permute-start = (bf16[128,1152]{1,0:T(8,128)(2,1)S(1)}, bf16[128,1152]{1,0:T(8,128)(2,1)}, u32[]{:S(2)}, u32[]{:S(2)}) collective-permute-start(bf16[128,1152]{1,0:T(8,128)(2,1)S(1)} %copy.29), channel_id=1, source_target_pairs={{0,4},{4,8},{8,12},{12,16},{16,20},{20,24},{24,28},{28,0},{1,5},{5... | collective-permute-start | bytes 884744 | tf_op jit(solution)/shard_map/while/body/eval_jaxpr/ppermute | solution.py:10
  290.8 14.6 %collective-permute-start.1 = (s32[128]{0:T(128)}, s32[128]{0:T(128)S(1)}, u32[]{:S(2)}, u32[]{:S(2)}) collective-permute-start(s32[128]{0:T(128)} %copy.30), channel_id=1, source_target_pairs={{0,4},{4,8},{8,12},{12,16},{16,20},{20,24},{24,28},{28,0},{1,5},{5... | collective-permute-start | bytes 1544 | tf_op jit(solution)/shard_map/while/body/eval_jaxpr/ppermute | solution.py:10
  311.3 14.6 %collective-permute-start.2 = (f32[128,1152]{1,0:T(8,128)}, f32[128,1152]{1,0:T(8,128)S(1)}, u32[]{:S(2)}, u32[]{:S(2)}) collective-permute-start(f32[128,1152]{1,0:T(8,128)} %convolution_add_fusion.5), channel_id=1, source_target_pairs={{0,4},{4,8},{8,12},{12,16},{16,20},{20,24},{24,28},{28,0},{1,5},{5... | collective-permute-start | bytes 1769480 | tf_op jit(solution)/shard_map/while/body/eval_jaxpr/ppermute | solution.py:10
  311.3 14.6 %collective-permute-start = (bf16[128,1152]{1,0:T(8,128)(2,1)S(1)}, bf16[128,1152]{1,0:T(8,128)(2,1)}, u32[]{:S(2)}, u32[]{:S(2)}) collective-permute-start(bf16[128,1152]{1,0:T(8,128)(2,1)S(1)} %copy.29), channel_id=1, source_target_pairs={{0,4},{4,8},{8,12},{12,16},{16,20},{20,24},{24,28},{28,0},{1,5},{5... | collective-permute-start | bytes 884744 | tf_op jit(solution)/shard_map/while/body/eval_jaxpr/ppermute | solution.py:10
  311.3 14.6 %collective-permute-start.1 = (s32[128]{0:T(128)}, s32[128]{0:T(128)S(1)}, u32[]{:S(2)}, u32[]{:S(2)}) collective-permute-start(s32[128]{0:T(128)} %copy.30), channel_id=1, source_target_pairs={{0,4},{4,8},{8,12},{12,16},{16,20},{20,24},{24,28},{28,0},{1,5},{5... | collective-permute-start | bytes 1544 | tf_op jit(solution)/shard_map/while/body/eval_jaxpr/ppermute | solution.py:10
  327.0 246.9 %all-reduce.5.cloned.1.call-start = ((), (), s32[]{:S(2)}) async-start(), calls=%async_computation.5 | async-start | bytes 21233664
  329.1 25.1 %copy-start.12 = (bf16[128,1152]{1,0:T(8,128)(2,1)S(1)}, bf16[128,1152]{1,0:T(8,128)(2,1)}, u32[]{:S(2)}) copy-start(bf16[128,1152]{1,0:T(8,128)(2,1)} %param.10) | copy-start | bytes 884740
  (27 other events, 114.3 us)
Sparse Core Ops, SparseCore 0:
  10.9 61.5 all-gather.10
  75.4 57.5 all-gather.8
  135.5 26.4 all-gather.6
  327.2 25.7 reduce-scatter.3
  359.3 214.6 all-reduce.4
where the time goes:
time: 585 us; the launch traced here: 584 us
  waiting for transfers between devices  462 us (79%)
  matrix products  62.5 us (11%)
  local copies, waits for them, and re-layouts  28.8 us (5%)
  between operations  14.6 us (2%)
  blocking collectives  7.88 us (1%)
    unnamed x6, waiting for transfers between devices  211 us
    ppermute x24, waiting for transfers between devices, passed_along(): return lax.ppermute(value, axis, pairs)  101 us
    all_gather x1, waiting for transfers between devices, on_device(): lax.all_gather(picture_mapping_matrix, ('dp', 'mp'), axis=0, tiled=True)  63.8 us
    all_gather x1, waiting for transfers between devices, on_device(): lax.all_gather(caption_mapping_matrix, ('dp', 'mp'), axis=0, tiled=True)  46.4 us
    dot_general x8, matrix products, pair_terms(): lax.dot_general(big_emb, text_emb, (((1,), (1,)), ((), ())), preferred_el...  24.7 us
    reduce_scatter x1, waiting for transfers between devices, on_device(): lax.psum_scatter(image_sum.astype(jnp.bfloat16), 'mp', scatter_dimension=...  20.5 us
    all_gather x1, waiting for transfers between devices, on_device(): lax.all_gather(emb_img, 'mp', axis=0, tiled=True)  19.6 us
    unnamed x33, local copies, waits for them, and re-layouts  16.1 us
  transfers between devices with their start and end apart: 29, of which 13 were waited for; matrix products, arithmetic and copies ran while one was open for 6% of the time, Pallas kernels for 0%

commit v1 on v0

v1 whole, which is shorter than its diff:
```python
import functools
import math

import jax
import jax.numpy as jnp
from jax import lax
from jax.experimental import pallas as pl
from jax.experimental.pallas import tpu as pltpu
from jax.sharding import PartitionSpec as P

MESH = pl.DeviceIdType.MESH
TXT, IMG = 0, 1
F32, BF16 = jnp.float32, jnp.bfloat16


def dot(a, b, da, db):
    return lax.dot_general(a, b, (((da,), (db,)), ((), ())), preferred_element_type=F32)


def loop(low, high, body):
    def step(i, carry):
        body(i)
        return carry

    lax.fori_loop(low, high, step, 0)


def kernel(
    nz, nm, rows, wrows,
    ximg, xtxt, wimg, wtxt, idimg, idtxt, sim_ref, off_ref,
    gimg, gtxt, dwimg, dwtxt,
    wbuf, wfull, fs, xt, unit, rad, dpre, imgs, txts, iids, tids, slopes,
    dt, tcs, tcr, tzs, tzr, dis, dir_, gown,
    rcs, rcr, rxs, rxr, rzs, rzr, rown,
    wz_s, wz_r, wx_s, wx_r, wc_s, wc_r,
    ii_s, ii_r, ti_s, ti_r, tj_s, tj_r,
    im_s, im_r, tx_s, tx_r, ty_s, ty_r,
    tc_s, tc_r, tz_s, tz_r, di_s, di_r,
    rc_s, rc_r, rx_s, rx_r, rz_s, rz_r,
):
    dp, m = lax.axis_index("dp"), lax.axis_index("mp")
    z, c = lax.div(dp, 2), lax.rem(dp, 2)
    other = 1 - c
    big = nm * wrows
    group = fs.shape[0] // big
    x_refs, w_refs = (xtxt, ximg), (wtxt, wimg)

    def zat(k):
        return lax.rem(z - k + nz, nz)

    def zto(k):
        return lax.rem(z + k, nz)

    def mat(k):
        return lax.rem(m - k + nm, nm)

    def mto(k):
        return lax.rem(m + k, nm)

    core = (2 * z + other, m)

    def copy(src, dst, s, r, dev):
        return pltpu.make_async_remote_copy(
            src_ref=src, dst_ref=dst, send_sem=s, recv_sem=r, device_id=dev, device_id_type=MESH
        )

    barrier = pltpu.get_barrier_semaphore()
    for k in range(1, nz):
        pl.semaphore_signal(barrier, inc=1, device_id=(2 * zto(k) + c, m), device_id_type=MESH)
    for k in range(1, nm):
        pl.semaphore_signal(barrier, inc=1, device_id=(dp, mto(k)), device_id_type=MESH)
    pl.semaphore_signal(barrier, inc=1, device_id=core, device_id_type=MESH)
    pl.semaphore_wait(barrier, nz + nm - 1)

    def w_z(w, k):
        return copy(w_refs[w], wbuf.at[w, dp, m], wz_s.at[w, k], wz_r.at[w, k], (2 * zto(k) + c, m))

    def w_x(w, k, j):
        slot = wbuf.at[w, 2 * zat(k) + c, m]
        return copy(slot, slot, wx_s.at[w, k, j], wx_r.at[w, k, j], (dp, mto(j)))

    def w_c(w, k, j):
        slot = wbuf.at[w, 2 * zat(k) + c, mat(j)]
        return copy(slot, slot, wc_s.at[w, k, j], wc_r.at[w, k, j], core)

    def w_z_wait(w, k):
        slot = wbuf.at[w, 2 * zat(k) + c, m]
        copy(slot, slot, wz_s.at[w, k], wz_r.at[w, k], core).wait_recv()

    def w_x_wait(w, k, j):
        slot = wbuf.at[w, 2 * zat(k) + c, mat(j)]
        copy(slot, slot, wx_s.at[w, k, j], wx_r.at[w, k, j], core).wait_recv()

    def w_c_wait(w, k, j):
        slot = wbuf.at[w, 2 * zat(k) + other, mat(j)]
        copy(slot, slot, wc_s.at[w, k, j], wc_r.at[w, k, j], core).wait_recv()

    def w_start(w):
        for k in range(1, nz):
            w_z(w, k).start()
        wbuf[w, dp, m] = w_refs[w][...]
        for j in range(1, nm):
            w_x(w, 0, j).start()
        w_c(w, 0, 0).start()

    def w_pass_z(w):
        def body(k):
            w_z_wait(w, k)
            for j in range(1, nm):
                w_x(w, k, j).start()
            w_c(w, k, 0).start()

        loop(1, nz, body)

    def w_pass_x(w):
        def body(k):
            for j in range(1, nm):
                w_x_wait(w, k, j)
                w_c(w, k, j).start()

        loop(0, nz, body)

    def w_finish(w):
        def body(k):
            for j in range(nm):
                w_c_wait(w, k, j)

        loop(0, nz, body)

        def join(g):
            for n in range(group * nm):
                d = g * group + n // nm
                fs[n * wrows:(n + 1) * wrows, :] = wbuf[w, d, n % nm].astype(F32)
            wfull[w, pl.ds(pl.multiple_of(g * group * big, 16), group * big), :] = fs[...].astype(BF16)

        loop(0, 2 * nz // group, join)

    def embed(w):
        pre = dot(x_refs[w][...], wfull[w], 1, 0)
        radius = jnp.sqrt(jnp.sum(pre * pre, axis=1, keepdims=True) + 1e-06)
        out = pre / radius
        unit[w] = out
        rad[w] = radius
        return out.astype(BF16)

    def my(n):
        return pl.ds(pl.multiple_of(n * rows, rows), rows)

    def ids_img(j):
        return copy(idimg, iids.at[m], ii_s.at[j], ii_r.at[j], (dp, mto(j)))

    def ids_txt(k):
        return copy(idtxt, tids.at[dp], ti_s.at[k], ti_r.at[k], (2 * zto(k) + c, m))

    def ids_core(k):
        slot = tids.at[2 * zat(k) + c]
        return copy(slot, slot, tj_s.at[k], tj_r.at[k], core)

    def img_x(j):
        slot = imgs.at[my(m), :]
        return copy(slot, slot, im_s.at[j], im_r.at[j], (dp, mto(j)))

    def txt_z(k):
        slot = txts.at[my(dp), :]
        return copy(slot, slot, tx_s.at[k], tx_r.at[k], (2 * zto(k) + c, m))

    def txt_c(k):
        slot = txts.at[my(2 * zat(k) + c), :]
        return copy(slot, slot, ty_s.at[k], ty_r.at[k], core)

    w_start(TXT)
    iids[m] = idimg[...]
    tids[dp] = idtxt[...]
    for j in range(1, nm):
        ids_img(j).start()
    for k in range(1, nz):
        ids_txt(k).start()
    ids_core(0).start()
    w_pass_z(TXT)
    w_start(IMG)
    for k in range(1, nz):
        slot = tids.at[2 * zat(k) + c]
        copy(slot, slot, ti_s.at[k], ti_r.at[k], core).wait_recv()
        ids_core(k).start()
    for w in (TXT, IMG):
        turned = x_refs[w][...].T if group == 1 else x_refs[w][...].astype(F32).T
        for d in range(2 * nz):
            xt[w, d] = turned[d * big:(d + 1) * big, :].astype(BF16)
    w_pass_x(TXT)
    w_pass_z(IMG)
    w_finish(TXT)
    txts[my(dp), :] = embed(TXT)
    txt_c(0).start()
    for k in range(1, nz):
        txt_z(k).start()
    w_pass_x(IMG)
    w_finish(IMG)
    imgs[my(m), :] = embed(IMG)
    for j in range(1, nm):
        img_x(j).start()

    for j in range(1, nm):
        slot = iids.at[mat(j)]
        copy(slot, slot, ii_s.at[j], ii_r.at[j], core).wait_recv()
    for k in range(nz):
        slot = tids.at[2 * zat(k) + other]
        copy(slot, slot, tj_s.at[k], tj_r.at[k], core).wait_recv()
    for j in range(1, nm):
        slot = imgs.at[my(mat(j)), :]
        copy(slot, slot, im_s.at[j], im_r.at[j], core).wait_recv()

    sim, off = sim_ref[0], off_ref[0]

    def grad_core(k):
        return copy(tcs.at[k], tcr.at[k], tc_s.at[k], tc_r.at[k], core)

    def grad_z(k):
        return copy(tzs.at[k], tzr.at[k], tz_s.at[k], tz_r.at[k], (2 * zat(k) + c, m))

    def pair(k):
        zs = zat(k)

        @pl.when(k > 0)
        def _():
            slot = txts.at[my(2 * zs + c), :]
            copy(slot, slot, tx_s.at[k], tx_r.at[k], core).wait_recv()
            txt_c(k).start()

        slot = txts.at[my(2 * zs + other), :]
        copy(slot, slot, ty_s.at[k], ty_r.at[k], core).wait_recv()
        span = pl.ds(pl.multiple_of(zs * 2 * rows, 2 * rows), 2 * rows)
        idrow = jnp.concatenate([tids[2 * zs][:1], tids[2 * zs + 1][:1]], axis=1)

        def block(q):
            here = my(q)
            logits = sim * dot(imgs[here, :], txts[span, :], 1, 1) + off
            idcol = iids[q].T[:, :1]
            sign = jnp.where(idcol == idrow, 1.0, -1.0).astype(F32)
            slopes[here, span] = (-sign * jax.nn.sigmoid(-sign * logits)).astype(BF16)

        loop(0, nm, block)
        for h in range(2):
            cols = pl.ds(pl.multiple_of(zs * 2 * rows + h * rows, rows), rows)
            dt[h] = dot(slopes[:, cols], imgs[...], 0, 0)
        tcs[k] = dt[other].astype(BF16)
        grad_core(k).start()
        grad_core(k).wait_recv()

        @pl.when(k > 0)
        def _():
            tzs[k] = (dt[c] + tcr[k].astype(F32)).astype(BF16)
            grad_z(k).start()

        @pl.when(k == 0)
        def _():
            gown[TXT] = dt[c] + tcr[k].astype(F32)

    loop(0, nz, pair)

    def grad_img(j):
        return copy(dis.at[j], dir_.at[j], di_s.at[j], di_r.at[j], (dp, mto(j)))

    def img_part(j):
        part = dot(slopes[my(mto(j)), :], txts[...], 1, 0)

        @pl.when(j < nm)
        def _():
            dis[j] = part.astype(BF16)
            grad_img(j).start()

        @pl.when(j == nm)
        def _():
            gown[IMG] = part

    loop(1, nm + 1, img_part)

    def rs_core(w, k):
        return copy(rcs.at[w, k], rcr.at[w, k], rc_s.at[w, k], rc_r.at[w, k], core)

    def rs_x(w, k, j):
        return copy(rxs.at[w, k, mto(j)], rxr.at[w, k, j], rx_s.at[w, k, j], rx_r.at[w, k, j], (dp, mto(j)))

    def rs_z(w, k):
        return copy(rzs.at[w, k], rzr.at[w, k], rz_s.at[w, k], rz_r.at[w, k], (2 * zto(k) + c, m))

    def w_part(w, d):
        return dot(xt[w, d], dpre[w], 1, 0)

    def backward(w, grad):
        u = unit[w]
        d = (grad - u * jnp.sum(u * grad, axis=1, keepdims=True)) / rad[w]
        dpre[w] = d.astype(BF16)

        def body(i):
            k = lax.rem(i, nz)
            rcs[w, k] = w_part(w, 2 * zto(k) + other).astype(BF16)
            rs_core(w, k).start()

        loop(1, nz + 1, body)

    def to_mp(w):
        def body(i):
            k = lax.rem(i, nz)
            rs_core(w, k).wait_recv()
            fs[:big, :] = w_part(w, 2 * zto(k) + c) + rcr[w, k].astype(F32)
            for q in range(nm):
                rxs[w, k, q] = fs[q * wrows:(q + 1) * wrows, :].astype(BF16)
            for j in range(1, nm):
                rs_x(w, k, j).start()

        loop(1, nz + 1, body)

    def to_z(w):
        def body(i):
            k = lax.rem(i, nz)
            total = rxs[w, k, m].astype(F32)
            for j in range(1, nm):
                rs_x(w, k, j).wait_recv()
                total = total + rxr[w, k, j].astype(F32)

            @pl.when(k > 0)
            def _():
                rzs[w, k] = total.astype(BF16)
                rs_z(w, k).start()

            @pl.when(k == 0)
            def _():
                rown[w] = total

        loop(1, nz + 1, body)

    def finish(w, out):
        total = rown[w]
        for k in range(1, nz):
            rs_z(w, k).wait_recv()
            total = total + rzr[w, k].astype(F32)
        out[...] = total

    grad = gown[IMG]
    for j in range(1, nm):
        grad_img(j).wait_recv()
        grad = grad + dir_[j].astype(F32)
    backward(IMG, sim * grad)
    gimg[...] = dot(dpre[IMG], wfull[IMG], 1, 1).astype(BF16)
    to_mp(IMG)
    grad = gown[TXT]
    for k in range(1, nz):
        grad_z(k).wait_recv()
        grad = grad + tzr[k].astype(F32)
    backward(TXT, sim * grad)
    to_mp(TXT)
    to_z(IMG)
    gtxt[...] = dot(dpre[TXT], wfull[TXT], 1, 1).astype(BF16)
    to_z(TXT)
    finish(IMG, dwimg)
    finish(TXT, dwtxt)

    for k in range(nz):
        ids_core(k).wait_send()
        txt_c(k).wait_send()
        grad_core(k).wait_send()
        if k > 0:
            ids_txt(k).wait_send()
            txt_z(k).wait_send()
            grad_z(k).wait_send()
    for j in range(1, nm):
        ids_img(j).wait_send()
        img_x(j).wait_send()
        grad_img(j).wait_send()
    for w in (TXT, IMG):
        def body(k):
            for j in range(nm):
                w_c(w, k, j).wait_send()
            rs_core(w, k).wait_send()
            for j in range(1, nm):
                w_x(w, k, j).wait_send()
                rs_x(w, k, j).wait_send()

            @pl.when(k > 0)
            def _():
                w_z(w, k).wait_send()
                rs_z(w, k).wait_send()

        loop(0, nz, body)


def call(nz, nm, args):
    ximg, xtxt, wimg, wtxt, idimg, idtxt, sim, off = args
    rows, depth = ximg.shape
    wrows, width = wimg.shape
    big = nm * wrows
    ndp = 2 * nz
    dma = pltpu.SemaphoreType.DMA
    vm = pltpu.VMEM
    sems = [
        dma((2, nz)), dma((2, nz)), dma((2, nz, nm)), dma((2, nz, nm)), dma((2, nz, nm)), dma((2, nz, nm)),
        dma((nm,)), dma((nm,)), dma((nz,)), dma((nz,)), dma((nz,)), dma((nz,)),
        dma((nm,)), dma((nm,)), dma((nz,)), dma((nz,)), dma((nz,)), dma((nz,)),
        dma((nz,)), dma((nz,)), dma((nz,)), dma((nz,)), dma((nm,)), dma((nm,)),
        dma((2, nz)), dma((2, nz)), dma((2, nz, nm)), dma((2, nz, nm)), dma((2, nz)), dma((2, nz)),
    ]
    scratch = [
        vm((2, ndp, nm, wrows, width), BF16),
        vm((2, depth, width), BF16),
        vm((math.lcm(big, 16), width), F32),
        vm((2, ndp, big, rows), BF16),
        vm((2, rows, width), F32),
        vm((2, rows, 1), F32),
        vm((2, rows, width), BF16),
        vm((nm * rows, width), BF16),
        vm((ndp * rows, width), BF16),
        vm((nm, 8, rows), jnp.int32),
        vm((ndp, 8, rows), jnp.int32),
        vm((nm * rows, ndp * rows), BF16),
        vm((2, rows, width), F32),
        vm((nz, rows, width), BF16),
        vm((nz, rows, width), BF16),
        vm((nz, rows, width), BF16),
        vm((nz, rows, width), BF16),
        vm((nm, rows, width), BF16),
        vm((nm, rows, width), BF16),
        vm((2, rows, width), F32),
        vm((2, nz, big, width), BF16),
        vm((2, nz, big, width), BF16),
        vm((2, nz, nm, wrows, width), BF16),
        vm((2, nz, nm, wrows, width), BF16),
        vm((2, nz, wrows, width), BF16),
        vm((2, nz, wrows, width), BF16),
        vm((2, wrows, width), F32),
    ]
    whole = pl.BlockSpec(memory_space=pltpu.VMEM)
    scalar = pl.BlockSpec(memory_space=pltpu.SMEM)
    return pl.pallas_call(
        functools.partial(kernel, nz, nm, rows, wrows),
        out_shape=(
            jax.ShapeDtypeStruct((rows, depth), BF16),
            jax.ShapeDtypeStruct((rows, depth), BF16),
            jax.ShapeDtypeStruct((wrows, width), F32),
            jax.ShapeDtypeStruct((wrows, width), F32),
        ),
        in_specs=[whole] * 6 + [scalar] * 2,
        out_specs=(whole,) * 4,
        scratch_shapes=scratch + sems,
        compiler_params=pltpu.CompilerParams(
            collective_id=0, has_side_effects=True, vmem_limit_bytes=62 * 1024 * 1024
        ),
        cost_estimate=pl.CostEstimate(flops=6 * 10**9, bytes_accessed=4 * 10**6, transcendentals=0),
    )(
        ximg, xtxt, wimg, wtxt,
        jnp.broadcast_to(idimg[None, :], (8, rows)), jnp.broadcast_to(idtxt[None, :], (8, rows)),
        sim, off,
    )


def solution(mesh):
    ndp, nm = mesh.shape["dp"], mesh.shape["mp"]

    def on_device(*args):
        return call(ndp // 2, nm, args)

    spec = P(("dp", "mp"), None)
    ids = P(("dp", "mp"))
    return jax.shard_map(
        on_device,
        mesh=mesh,
        in_specs=(spec, spec, spec, spec, ids, ids, P(), P()),
        out_specs=(spec,) * 4,
        check_vma=False,
    )
```

time: 585 us -> 139 us (0.24)
  waiting for transfers between devices: 462 us -> 0 us
  Pallas kernels: 0 us -> 131 us
  matrix products: 62.5 us -> 0 us
  local copies, waits for them, and re-layouts: 28.8 us -> 5.69 us
  between operations: 14.6 us -> 1.98 us
  blocking collectives: 7.88 us -> 0 us
    unnamed x6 -> x0, waiting for transfers between devices: 211 us -> none
    pallas_call x0 -> x1, Pallas kernels: none -> 131 us  [call(): pl.pallas_call(functools.partial(kernel, nz, nm, rows, wrows), out_shape=...]
    all_gather x3 -> x0, waiting for transfers between devices: 130 us -> none  [the longest x1 63.8 us: on_device(): lax.all_gather(picture_mapping_matrix, ('dp', 'mp'), axis=0, tiled=True)]
    ppermute x24 -> x0, waiting for transfers between devices: 101 us -> none  [passed_along(): return lax.ppermute(value, axis, pairs)]
    dot_general x30 -> x0, matrix products: 62.5 us -> none  [the longest x8 24.7 us: pair_terms(): lax.dot_general(big_emb, text_emb, (((1,), (1,)), ((), ())), preferred_el...]
    reduce_scatter x1 -> x0, waiting for transfers between devices: 20.5 us -> none  [on_device(): lax.psum_scatter(image_sum.astype(jnp.bfloat16), 'mp', scatter_dimension=...]
    while x48 -> x0, local copies, waits for them, and re-layouts: 12.6 us -> none
    unnamed x33 -> x14, local copies, waits for them, and re-layouts: 16.1 us -> 4.5 us
  transfers between devices with their start and end apart: 29 -> 0, of which waited for: 13 -> 0; matrix products, arithmetic and copies ran while one was open for 6% -> 0% of each run, Pallas kernels for 0% -> 0%
where the time goes in v1:
time: 139 us
  Pallas kernels  131 us (94%)
  local copies, waits for them, and re-layouts  5.69 us (4%)
  between operations  1.98 us (1%)
    pallas_call x1, Pallas kernels, call(): pl.pallas_call(functools.partial(kernel, nz, nm, rows, wrows), out_shape=...  131 us
    unnamed x14, local copies, waits for them, and re-layouts  4.5 us

profile of v1, /device:TPU:0, one launch (start us, length us, event | category | flops | bytes accessed | tf_op | source)
XLA Modules:
  0.0 138.8 jit_solution(16821090796736747641)
XLA Ops:
  1.3 0.0 copy-start.3
  1.9 0.0 copy-done.3
  2.0 0.0 copy-start.4
  2.0 0.6 broadcast_in_dim.4.idimg
  2.6 0.1 copy-done.4
  2.6 0.6 broadcast_in_dim.5.idtxt
  3.2 131.1 %shard_map.111 = (bf16[128,1152]{1,0:T(8,128)(2,1)}, bf16[128,1152]{1,0:T(8,128)(2,1)}, f32[36,1152]{1,0:T(8,128)}, f32[36,1152]{1,0:T(8,128)}) custom-call(bf16[128,1152]{1,0:T(8,128)(2,1)} %ximg.1, bf16[128,1152]{1,0:T(8,128)(2,1)} %xtxt.1, bf16[36,1152]{1,0:T(8,128)(2,1)} %wimg.1, bf16[36,1152]{1,0:T(8,128)(2,1)} %wtxt.1, ...), custom_call_target="tpu_custom_call" | custom-call | flops 6000000000 | bytes 4000000 | tf_op jit(solution)/shard_map/pallas_call | solution.py:433
  134.4 0.0 copy-start
  134.4 1.7 %copy.18 = bf16[128,1152]{1,0:T(8,128)(2,1)} copy(bf16[128,1152]{1,0:T(8,128)(2,1)} %get-tuple-element.8) | data formatting | bytes 589824
  136.1 0.0 copy-done
  136.1 0.0 copy-start.2
  136.1 0.7 copy.19
  136.8 0.3 copy-done.2
  137.1 0.0 copy-start.1
  137.1 0.7 copy.20
  137.8 0.3 copy-done.1
  138.1 0.7 copy.21
Async XLA Ops:
  1.3 0.7 copy-start.3
  2.0 0.7 copy-start.4
  134.4 1.8 %copy-start = (bf16[128,1152]{1,0:T(8,128)(2,1)S(1)}, bf16[128,1152]{1,0:T(8,128)(2,1)}, u32[]{:S(2)}) copy-start(bf16[128,1152]{1,0:T(8,128)(2,1)} %get-tuple-element.9) | copy-start | bytes 884740
  136.1 1.0 copy-start.2
  137.1 1.0 copy-start.1

commit v2 on v1

--- a/solution.py
+++ b/solution.py
@@ -31,7 +31,7 @@
     gimg, gtxt, dwimg, dwtxt,
     wbuf, wfull, fs, xt, unit, rad, dpre, imgs, txts, iids, tids, slopes,
     dt, tcs, tcr, tzs, tzr, dis, dir_, gown,
-    rcs, rcr, rxs, rxr, rzs, rzr, rown,
+    rcs, rcr, rxs, rxr, rys, ryr, rzs, rzr, rown,
     wz_s, wz_r, wx_s, wx_r, wc_s, wc_r,
     ii_s, ii_r, ti_s, ti_r, tj_s, tj_r,
     im_s, im_r, tx_s, tx_r, ty_s, ty_r,
@@ -58,6 +58,19 @@
         return lax.rem(m + k, nm)
 
     core = (2 * z + other, m)
+    square = nm == 4
+    xbit, ybit = lax.rem(m, 2), lax.div(m, 2)
+    across = (m, m + 1 - 2 * xbit, m + 2 - 4 * ybit, 3 - m)
+    near = (1, 2) if square else range(1, nm)
+
+    def whom(j):
+        return across[j] if square else mto(j)
+
+    def whose(j):
+        return across[j] if square else mat(j)
+
+    def pick(k, even, odd):
+        return even + lax.rem(k, 2) * (odd - even)
 
     def copy(src, dst, s, r, dev):
         return pltpu.make_async_remote_copy(
@@ -77,10 +90,14 @@
 
     def w_x(w, k, j):
         slot = wbuf.at[w, 2 * zat(k) + c, m]
-        return copy(slot, slot, wx_s.at[w, k, j], wx_r.at[w, k, j], (dp, mto(j)))
+        return copy(slot, slot, wx_s.at[w, k, j], wx_r.at[w, k, j], (dp, whom(j)))
+
+    def w_diag(w, k):
+        slot = wbuf.at[w, 2 * zat(k) + c, pick(k, across[1], across[2])]
+        return copy(slot, slot, wx_s.at[w, k, 3], wx_r.at[w, k, 3], (dp, pick(k, across[2], across[1])))
 
     def w_c(w, k, j):
-        slot = wbuf.at[w, 2 * zat(k) + c, mat(j)]
+        slot = wbuf.at[w, 2 * zat(k) + c, whose(j)]
         return copy(slot, slot, wc_s.at[w, k, j], wc_r.at[w, k, j], core)
 
     def w_z_wait(w, k):
@@ -88,25 +105,25 @@
         copy(slot, slot, wz_s.at[w, k], wz_r.at[w, k], core).wait_recv()
 
     def w_x_wait(w, k, j):
-        slot = wbuf.at[w, 2 * zat(k) + c, mat(j)]
+        slot = wbuf.at[w, 2 * zat(k) + c, whose(j)]
         copy(slot, slot, wx_s.at[w, k, j], wx_r.at[w, k, j], core).wait_recv()
 
     def w_c_wait(w, k, j):
-        slot = wbuf.at[w, 2 * zat(k) + other, mat(j)]
+        slot = wbuf.at[w, 2 * zat(k) + other, whose(j)]
         copy(slot, slot, wc_s.at[w, k, j], wc_r.at[w, k, j], core).wait_recv()
 
     def w_start(w):
         for k in range(1, nz):
             w_z(w, k).start()
         wbuf[w, dp, m] = w_refs[w][...]
-        for j in range(1, nm):
+        for j in near:
             w_x(w, 0, j).start()
         w_c(w, 0, 0).start()
 
     def w_pass_z(w):
         def body(k):
             w_z_wait(w, k)
-            for j in range(1, nm):
+            for j in near:
                 w_x(w, k, j).start()
             w_c(w, k, 0).start()
 
@@ -114,26 +131,45 @@
 
     def w_pass_x(w):
         def body(k):
-            for j in range(1, nm):
+            for j in near:
                 w_x_wait(w, k, j)
                 w_c(w, k, j).start()
+            if square:
+                w_diag(w, k).start()
 
         loop(0, nz, body)
 
+    def join(w, d):
+        for q in range(nm):
+            fs[q * wrows:(q + 1) * wrows, :] = wbuf[w, d, q].astype(F32)
+        wfull[w, pl.ds(pl.multiple_of(d * big, 16), big), :] = fs[...].astype(BF16)
+
     def w_finish(w):
-        def body(k):
+        def own(k):
+            if square:
+                w_x_wait(w, k, 3)
+                w_c(w, k, 3).start()
+            if group == 1:
+                join(w, 2 * zat(k) + c)
+
+        loop(0, nz, own)
+
+        def rest(k):
             for j in range(nm):
                 w_c_wait(w, k, j)
-
-        loop(0, nz, body)
-
-        def join(g):
+            if group == 1:
+                join(w, 2 * zat(k) + other)
+
+        loop(0, nz, rest)
+
+        def join_group(g):
             for n in range(group * nm):
                 d = g * group + n // nm
                 fs[n * wrows:(n + 1) * wrows, :] = wbuf[w, d, n % nm].astype(F32)
             wfull[w, pl.ds(pl.multiple_of(g * group * big, 16), group * big), :] = fs[...].astype(BF16)
 
-        loop(0, 2 * nz // group, join)
+        if group > 1:
+            loop(0, 2 * nz // group, join_group)
 
     def embed(w):
         pre = dot(x_refs[w][...], wfull[w], 1, 0)
@@ -147,10 +183,10 @@
         return pl.ds(pl.multiple_of(n * rows, rows), rows)
 
     def ids_img(j):
-        return copy(idimg, iids.at[m], ii_s.at[j], ii_r.at[j], (dp, mto(j)))
+        return copy(iids.at[m], iids.at[m], ii_s.at[j], ii_r.at[j], (dp, mto(j)))
 
     def ids_txt(k):
-        return copy(idtxt, tids.at[dp], ti_s.at[k], ti_r.at[k], (2 * zto(k) + c, m))
+        return copy(tids.at[dp], tids.at[dp], ti_s.at[k], ti_r.at[k], (2 * zto(k) + c, m))
 
     def ids_core(k):
         slot = tids.at[2 * zat(k) + c]
@@ -168,16 +204,17 @@
         slot = txts.at[my(2 * zat(k) + c), :]
         return copy(slot, slot, ty_s.at[k], ty_r.at[k], core)
 
-    w_start(TXT)
-    iids[m] = idimg[...]
-    tids[dp] = idtxt[...]
+    w_start(IMG)
+    iids[m] = jnp.broadcast_to(idimg[...], (8, rows))
+    tids[dp] = jnp.broadcast_to(idtxt[...], (8, rows))
     for j in range(1, nm):
         ids_img(j).start()
     for k in range(1, nz):
         ids_txt(k).start()
     ids_core(0).start()
-    w_pass_z(TXT)
-    w_start(IMG)
+    w_pass_z(IMG)
+    w_start(TXT)
+    w_pass_x(IMG)
     for k in range(1, nz):
         slot = tids.at[2 * zat(k) + c]
         copy(slot, slot, ti_s.at[k], ti_r.at[k], core).wait_recv()
@@ -186,18 +223,17 @@
         turned = x_refs[w][...].T if group == 1 else x_refs[w][...].astype(F32).T
         for d in range(2 * nz):
             xt[w, d] = turned[d * big:(d + 1) * big, :].astype(BF16)
+    w_pass_z(TXT)
+    w_finish(IMG)
+    imgs[my(m), :] = embed(IMG)
+    for j in range(1, nm):
+        img_x(j).start()
     w_pass_x(TXT)
-    w_pass_z(IMG)
     w_finish(TXT)
     txts[my(dp), :] = embed(TXT)
     txt_c(0).start()
     for k in range(1, nz):
         txt_z(k).start()
-    w_pass_x(IMG)
-    w_finish(IMG)
-    imgs[my(m), :] = embed(IMG)
-    for j in range(1, nm):
-        img_x(j).start()
 
     for j in range(1, nm):
         slot = iids.at[mat(j)]
@@ -231,17 +267,14 @@
         span = pl.ds(pl.multiple_of(zs * 2 * rows, 2 * rows), 2 * rows)
         idrow = jnp.concatenate([tids[2 * zs][:1], tids[2 * zs + 1][:1]], axis=1)
 
-        def block(q):
-            here = my(q)
-            logits = sim * dot(imgs[here, :], txts[span, :], 1, 1) + off
-            idcol = iids[q].T[:, :1]
-            sign = jnp.where(idcol == idrow, 1.0, -1.0).astype(F32)
-            slopes[here, span] = (-sign * jax.nn.sigmoid(-sign * logits)).astype(BF16)
-
-        loop(0, nm, block)
+        logits = sim * dot(imgs[...], txts[span, :], 1, 1) + off
+        idcol = jnp.concatenate([iids[q].T[:, :1] for q in range(nm)], axis=0)
+        sign = jnp.where(idcol == idrow, 1.0, -1.0).astype(F32)
+        slope = (-sign * jax.nn.sigmoid(-sign * logits)).astype(BF16)
+        slopes[:, span] = slope
+        part = dot(slope, imgs[...], 0, 0)
         for h in range(2):
-            cols = pl.ds(pl.multiple_of(zs * 2 * rows + h * rows, rows), rows)
-            dt[h] = dot(slopes[:, cols], imgs[...], 0, 0)
+            dt[h] = part[h * rows:(h + 1) * rows, :]
         tcs[k] = dt[other].astype(BF16)
         grad_core(k).start()
         grad_core(k).wait_recv()
@@ -277,8 +310,16 @@
     def rs_core(w, k):
         return copy(rcs.at[w, k], rcr.at[w, k], rc_s.at[w, k], rc_r.at[w, k], core)
 
-    def rs_x(w, k, j):
+    def rs_x(w, k):
+        there = (dp, pick(k, across[1], across[2]))
+        return copy(rxs.at[w, k, pl.ds(2, 2)], rxr.at[w, k], rx_s.at[w, k, 0], rx_r.at[w, k, 0], there)
+
+    def rs_far(w, k, j):
         return copy(rxs.at[w, k, mto(j)], rxr.at[w, k, j], rx_s.at[w, k, j], rx_r.at[w, k, j], (dp, mto(j)))
+
+    def rs_y(w, k):
+        there = (dp, pick(k, across[2], across[1]))
+        return copy(rys.at[w, k], ryr.at[w, k], rx_s.at[w, k, 1], rx_r.at[w, k, 1], there)
 
     def rs_z(w, k):
         return copy(rzs.at[w, k], rzr.at[w, k], rz_s.at[w, k], rz_r.at[w, k], (2 * zto(k) + c, m))
@@ -304,19 +345,38 @@
             rs_core(w, k).wait_recv()
             fs[:big, :] = w_part(w, 2 * zto(k) + c) + rcr[w, k].astype(F32)
             for q in range(nm):
-                rxs[w, k, q] = fs[q * wrows:(q + 1) * wrows, :].astype(BF16)
-            for j in range(1, nm):
-                rs_x(w, k, j).start()
+                dx, dy = lax.rem(xbit + q % 2, 2), lax.rem(ybit + q // 2, 2)
+                place = pick(k, 2 * dx + dy, 2 * dy + dx) if square else q
+                rxs[w, k, place] = fs[q * wrows:(q + 1) * wrows, :].astype(BF16)
+            if square:
+                rs_x(w, k).start()
+            else:
+                for j in near:
+                    rs_far(w, k, j).start()
 
         loop(1, nz + 1, body)
+
+    def to_y(w):
+        def body(i):
+            k = lax.rem(i, nz)
+            rs_x(w, k).wait_recv()
+            rys[w, k] = (rxs[w, k, 1].astype(F32) + rxr[w, k, 1].astype(F32)).astype(BF16)
+            rs_y(w, k).start()
+
+        if square:
+            loop(1, nz + 1, body)
 
     def to_z(w):
         def body(i):
             k = lax.rem(i, nz)
-            total = rxs[w, k, m].astype(F32)
-            for j in range(1, nm):
-                rs_x(w, k, j).wait_recv()
-                total = total + rxr[w, k, j].astype(F32)
+            if square:
+                rs_y(w, k).wait_recv()
+                total = rxs[w, k, 0].astype(F32) + rxr[w, k, 0].astype(F32) + ryr[w, k].astype(F32)
+            else:
+                total = rxs[w, k, m].astype(F32)
+                for j in near:
+                    rs_far(w, k, j).wait_recv()
+                    total = total + rxr[w, k, j].astype(F32)
 
             @pl.when(k > 0)
             def _():
@@ -343,6 +403,7 @@
     backward(IMG, sim * grad)
     gimg[...] = dot(dpre[IMG], wfull[IMG], 1, 1).astype(BF16)
     to_mp(IMG)
+    to_y(IMG)
     grad = gown[TXT]
     for k in range(1, nz):
         grad_z(k).wait_recv()
@@ -350,6 +411,7 @@
     backward(TXT, sim * grad)
     to_mp(TXT)
     to_z(IMG)
+    to_y(TXT)
     gtxt[...] = dot(dpre[TXT], wfull[TXT], 1, 1).astype(BF16)
     to_z(TXT)
     finish(IMG, dwimg)
@@ -372,9 +434,15 @@
             for j in range(nm):
                 w_c(w, k, j).wait_send()
             rs_core(w, k).wait_send()
-            for j in range(1, nm):
+            for j in near:
                 w_x(w, k, j).wait_send()
-                rs_x(w, k, j).wait_send()
+            if square:
+                w_diag(w, k).wait_send()
+                rs_x(w, k).wait_send()
+                rs_y(w, k).wait_send()
+            else:
+                for j in near:
+                    rs_far(w, k, j).wait_send()
 
             @pl.when(k > 0)
             def _():
@@ -423,7 +491,9 @@
         vm((2, nz, big, width), BF16),
         vm((2, nz, big, width), BF16),
         vm((2, nz, nm, wrows, width), BF16),
-        vm((2, nz, nm, wrows, width), BF16),
+        vm((2, nz, 2 if nm == 4 else nm, wrows, width), BF16),
+        vm((2, nz, wrows, width), BF16),
+        vm((2, nz, wrows, width), BF16),
         vm((2, nz, wrows, width), BF16),
         vm((2, nz, wrows, width), BF16),
         vm((2, wrows, width), F32),
@@ -447,7 +517,7 @@
         cost_estimate=pl.CostEstimate(flops=6 * 10**9, bytes_accessed=4 * 10**6, transcendentals=0),
     )(
         ximg, xtxt, wimg, wtxt,
-        jnp.broadcast_to(idimg[None, :], (8, rows)), jnp.broadcast_to(idtxt[None, :], (8, rows)),
+        idimg[None, :], idtxt[None, :],
         sim, off,
     )
 

time: 139 us -> 158 us (1.14)
  Pallas kernels: 131 us -> 151 us
    pallas_call x1, Pallas kernels: 131 us -> 151 us  [call(): pl.pallas_call(functools.partial(kernel, nz, nm, rows, wrows), out_shape=...]
    unnamed x14 -> x10, local copies, waits for them, and re-layouts: 4.5 us -> 4.44 us
where the time goes in v2:
time: 158 us
  Pallas kernels  151 us (96%)
  local copies, waits for them, and re-layouts  4.44 us (3%)
  between operations  1.94 us (1%)
    pallas_call x1, Pallas kernels, call(): pl.pallas_call(functools.partial(kernel, nz, nm, rows, wrows), out_shape=...  151 us
    unnamed x10, local copies, waits for them, and re-layouts  4.44 us

profile of v2, /device:TPU:0, one launch (start us, length us, event | category | flops | bytes accessed | tf_op | source)
XLA Modules:
  0.0 157.8 jit_solution(14296215961554793988)
XLA Ops:
  1.9 151.4 %shard_map.111 = (bf16[128,1152]{1,0:T(8,128)(2,1)}, bf16[128,1152]{1,0:T(8,128)(2,1)}, f32[36,1152]{1,0:T(8,128)}, f32[36,1152]{1,0:T(8,128)}) custom-call(bf16[128,1152]{1,0:T(8,128)(2,1)} %ximg.1, bf16[128,1152]{1,0:T(8,128)(2,1)} %xtxt.1, bf16[36,1152]{1,0:T(8,128)(2,1)} %wimg.1, bf16[36,1152]{1,0:T(8,128)(2,1)} %wtxt.1, s32[1,128]{1,0:T(1,128)} %bitcast.2, ...), custom_call_target="tpu_custom_call" | custom-call | flops 6000000000 | bytes 4000000 | tf_op jit(solution)/shard_map/pallas_call | solution.py:503
  153.4 0.0 copy-start
  153.4 1.7 %copy.18 = bf16[128,1152]{1,0:T(8,128)(2,1)} copy(bf16[128,1152]{1,0:T(8,128)(2,1)} %get-tuple-element.8) | data formatting | bytes 589824
  155.1 0.0 copy-done
  155.1 0.0 copy-start.2
  155.1 0.7 copy.19
  155.8 0.3 copy-done.2
  156.2 0.0 copy-start.1
  156.2 0.7 copy.20
  156.8 0.3 copy-done.1
  157.1 0.7 copy.21
Async XLA Ops:
  153.4 1.8 %copy-start = (bf16[128,1152]{1,0:T(8,128)(2,1)S(1)}, bf16[128,1152]{1,0:T(8,128)(2,1)}, u32[]{:S(2)}) copy-start(bf16[128,1152]{1,0:T(8,128)(2,1)} %get-tuple-element.9) | copy-start | bytes 884740
  155.1 1.0 copy-start.2
  156.2 1.0 copy-start.1

commit v3 on v2

--- a/solution.py
+++ b/solution.py
@@ -204,7 +204,7 @@
         slot = txts.at[my(2 * zat(k) + c), :]
         return copy(slot, slot, ty_s.at[k], ty_r.at[k], core)
 
-    w_start(IMG)
+    w_start(TXT)
     iids[m] = jnp.broadcast_to(idimg[...], (8, rows))
     tids[dp] = jnp.broadcast_to(idtxt[...], (8, rows))
     for j in range(1, nm):
@@ -212,9 +212,9 @@
     for k in range(1, nz):
         ids_txt(k).start()
     ids_core(0).start()
-    w_pass_z(IMG)
-    w_start(TXT)
-    w_pass_x(IMG)
+    w_pass_z(TXT)
+    w_start(IMG)
+    w_pass_x(TXT)
     for k in range(1, nz):
         slot = tids.at[2 * zat(k) + c]
         copy(slot, slot, ti_s.at[k], ti_r.at[k], core).wait_recv()
@@ -223,18 +223,24 @@
         turned = x_refs[w][...].T if group == 1 else x_refs[w][...].astype(F32).T
         for d in range(2 * nz):
             xt[w, d] = turned[d * big:(d + 1) * big, :].astype(BF16)
-    w_pass_z(TXT)
+    w_pass_z(IMG)
+    w_finish(TXT)
+    txts[my(dp), :] = embed(TXT)
+    for k in range(1, nz):
+        txt_z(k).start()
+    txt_c(0).start()
+    w_pass_x(IMG)
     w_finish(IMG)
     imgs[my(m), :] = embed(IMG)
     for j in range(1, nm):
         img_x(j).start()
-    w_pass_x(TXT)
-    w_finish(TXT)
-    txts[my(dp), :] = embed(TXT)
-    txt_c(0).start()
-    for k in range(1, nz):
-        txt_z(k).start()
-
+
+    def take_txt(k):
+        slot = txts.at[my(2 * zat(k) + c), :]
+        copy(slot, slot, tx_s.at[k], tx_r.at[k], core).wait_recv()
+        txt_c(k).start()
+
+    loop(1, nz, take_txt)
     for j in range(1, nm):
         slot = iids.at[mat(j)]
         copy(slot, slot, ii_s.at[j], ii_r.at[j], core).wait_recv()
@@ -253,14 +259,9 @@
     def grad_z(k):
         return copy(tzs.at[k], tzr.at[k], tz_s.at[k], tz_r.at[k], (2 * zat(k) + c, m))
 
-    def pair(k):
+    def pair(i):
+        k = lax.rem(i, nz)
         zs = zat(k)
-
-        @pl.when(k > 0)
-        def _():
-            slot = txts.at[my(2 * zs + c), :]
-            copy(slot, slot, tx_s.at[k], tx_r.at[k], core).wait_recv()
-            txt_c(k).start()
 
         slot = txts.at[my(2 * zs + other), :]
         copy(slot, slot, ty_s.at[k], ty_r.at[k], core).wait_recv()
@@ -288,7 +289,7 @@
         def _():
             gown[TXT] = dt[c] + tcr[k].astype(F32)
 
-    loop(0, nz, pair)
+    loop(1, nz + 1, pair)
 
     def grad_img(j):
         return copy(dis.at[j], dir_.at[j], di_s.at[j], di_r.at[j], (dp, mto(j)))

time: 158 us -> 130 us (0.82)
  Pallas kernels: 151 us -> 124 us
    pallas_call x1, Pallas kernels: 151 us -> 124 us  [call(): pl.pallas_call(functools.partial(kernel, nz, nm, rows, wrows), out_shape=...]
where the time goes in v3:
time: 130 us
  Pallas kernels  124 us (95%)
  local copies, waits for them, and re-layouts  4.44 us (3%)
  between operations  1.94 us (1%)
    pallas_call x1, Pallas kernels, call(): pl.pallas_call(functools.partial(kernel, nz, nm, rows, wrows), out_shape=...  124 us
    unnamed x10, local copies, waits for them, and re-layouts  4.44 us

profile of v3, /device:TPU:0, one launch (start us, length us, event | category | flops | bytes accessed | tf_op | source)
XLA Modules:
  0.0 130.0 jit_solution(7827588650786361596)
XLA Ops:
  1.9 123.6 %shard_map.111 = (bf16[128,1152]{1,0:T(8,128)(2,1)}, bf16[128,1152]{1,0:T(8,128)(2,1)}, f32[36,1152]{1,0:T(8,128)}, f32[36,1152]{1,0:T(8,128)}) custom-call(bf16[128,1152]{1,0:T(8,128)(2,1)} %ximg.1, bf16[128,1152]{1,0:T(8,128)(2,1)} %xtxt.1, bf16[36,1152]{1,0:T(8,128)(2,1)} %wimg.1, bf16[36,1152]{1,0:T(8,128)(2,1)} %wtxt.1, s32[1,128]{1,0:T(1,128)} %bitcast.2, ...), custom_call_target="tpu_custom_call" | custom-call | flops 6000000000 | bytes 4000000 | tf_op jit(solution)/shard_map/pallas_call | solution.py:504
  125.5 0.0 copy-start
  125.6 1.7 %copy.18 = bf16[128,1152]{1,0:T(8,128)(2,1)} copy(bf16[128,1152]{1,0:T(8,128)(2,1)} %get-tuple-element.8) | data formatting | bytes 589824
  127.3 0.0 copy-done
  127.3 0.0 copy-start.2
  127.3 0.7 copy.19
  128.0 0.3 copy-done.2
  128.3 0.0 copy-start.1
  128.3 0.7 copy.20
  129.0 0.3 copy-done.1
  129.3 0.7 copy.21
Async XLA Ops:
  125.5 1.8 %copy-start = (bf16[128,1152]{1,0:T(8,128)(2,1)S(1)}, bf16[128,1152]{1,0:T(8,128)(2,1)}, u32[]{:S(2)}) copy-start(bf16[128,1152]{1,0:T(8,128)(2,1)} %get-tuple-element.9) | copy-start | bytes 884740
  127.3 1.0 copy-start.2
  128.3 1.0 copy-start.1

commit v4 on v3

--- a/solution.py
+++ b/solution.py
@@ -57,6 +57,14 @@
     def mto(k):
         return lax.rem(m + k, nm)
 
+    line = nz == 4
+
+    def beyond(k):
+        return lax.rem(z + k, 2) + 2 * lax.rem(lax.div(z, 2) + lax.div(k, 2), 2)
+
+    def zof(k):
+        return beyond(k) if line else zat(k)
+
     core = (2 * z + other, m)
     square = nm == 4
     xbit, ybit = lax.rem(m, 2), lax.div(m, 2)
@@ -198,10 +206,15 @@
 
     def txt_z(k):
         slot = txts.at[my(dp), :]
-        return copy(slot, slot, tx_s.at[k], tx_r.at[k], (2 * zto(k) + c, m))
+        there = beyond(k) if line else zto(k)
+        return copy(slot, slot, tx_s.at[k], tx_r.at[k], (2 * there + c, m))
+
+    def txt_on():
+        slot = txts.at[my(2 * beyond(2) + c), :]
+        return copy(slot, slot, tx_s.at[3], tx_r.at[3], (2 * beyond(1) + c, m))
 
     def txt_c(k):
-        slot = txts.at[my(2 * zat(k) + c), :]
+        slot = txts.at[my(2 * zof(k) + c), :]
         return copy(slot, slot, ty_s.at[k], ty_r.at[k], core)
 
     w_start(TXT)
@@ -226,7 +239,7 @@
     w_pass_z(IMG)
     w_finish(TXT)
     txts[my(dp), :] = embed(TXT)
-    for k in range(1, nz):
+    for k in (2, 1) if line else range(1, nz):
         txt_z(k).start()
     txt_c(0).start()
     w_pass_x(IMG)
@@ -235,12 +248,13 @@
     for j in range(1, nm):
         img_x(j).start()
 
-    def take_txt(k):
-        slot = txts.at[my(2 * zat(k) + c), :]
+    for k in (2, 1, 3) if line else range(1, nz):
+        slot = txts.at[my(2 * zof(k) + c), :]
         copy(slot, slot, tx_s.at[k], tx_r.at[k], core).wait_recv()
+        if line and k == 2:
+            txt_on().start()
         txt_c(k).start()
 
-    loop(1, nz, take_txt)
     for j in range(1, nm):
         slot = iids.at[mat(j)]
         copy(slot, slot, ii_s.at[j], ii_r.at[j], core).wait_recv()
@@ -257,11 +271,15 @@
         return copy(tcs.at[k], tcr.at[k], tc_s.at[k], tc_r.at[k], core)
 
     def grad_z(k):
-        return copy(tzs.at[k], tzr.at[k], tz_s.at[k], tz_r.at[k], (2 * zat(k) + c, m))
+        there = pick(k, beyond(2), beyond(1)) if line else zat(k)
+        return copy(tzs.at[k], tzr.at[k], tz_s.at[k], tz_r.at[k], (2 * there + c, m))
 
     def pair(i):
-        k = lax.rem(i, nz)
-        zs = zat(k)
+        if line:
+            k = 3 - 2 * lax.div(i + 1, 2) + lax.div(i, 2)
+        else:
+            k = lax.rem(i + 1, nz)
+        zs = zof(k)
 
         slot = txts.at[my(2 * zs + other), :]
         copy(slot, slot, ty_s.at[k], ty_r.at[k], core).wait_recv()
@@ -280,16 +298,19 @@
         grad_core(k).start()
         grad_core(k).wait_recv()
 
+        gown[TXT] = dt[c] + tcr[k].astype(F32)
+        if line:
+            @pl.when(k == 2)
+            def _():
+                grad_z(3).wait_recv()
+                gown[TXT] = gown[TXT] + tzr[3].astype(F32)
+
         @pl.when(k > 0)
         def _():
-            tzs[k] = (dt[c] + tcr[k].astype(F32)).astype(BF16)
+            tzs[k] = gown[TXT].astype(BF16)
             grad_z(k).start()
 
-        @pl.when(k == 0)
-        def _():
-            gown[TXT] = dt[c] + tcr[k].astype(F32)
-
-    loop(1, nz + 1, pair)
+    loop(0, nz, pair)
 
     def grad_img(j):
         return copy(dis.at[j], dir_.at[j], di_s.at[j], di_r.at[j], (dp, mto(j)))
@@ -406,7 +427,7 @@
     to_mp(IMG)
     to_y(IMG)
     grad = gown[TXT]
-    for k in range(1, nz):
+    for k in (1, 2) if line else range(1, nz):
         grad_z(k).wait_recv()
         grad = grad + tzr[k].astype(F32)
     backward(TXT, sim * grad)
@@ -424,7 +445,10 @@
         grad_core(k).wait_send()
         if k > 0:
             ids_txt(k).wait_send()
-            txt_z(k).wait_send()
+            if line and k == 3:
+                txt_on().wait_send()
+            else:
+                txt_z(k).wait_send()
             grad_z(k).wait_send()
     for j in range(1, nm):
         ids_img(j).wait_send()

time: 130 us -> 133 us (1.023)
  Pallas kernels: 124 us -> 126 us
    pallas_call x1, Pallas kernels: 124 us -> 126 us  [call(): pl.pallas_call(functools.partial(kernel, nz, nm, rows, wrows), out_shape=...]
where the time goes in v4:
time: 133 us
  Pallas kernels  126 us (95%)
  local copies, waits for them, and re-layouts  4.44 us (3%)
  between operations  1.94 us (1%)
    pallas_call x1, Pallas kernels, call(): pl.pallas_call(functools.partial(kernel, nz, nm, rows, wrows), out_shape=...  126 us
    unnamed x10, local copies, waits for them, and re-layouts  4.44 us

profile of v4, /device:TPU:0, one launch (start us, length us, event | category | flops | bytes accessed | tf_op | source)
XLA Modules:
  0.0 132.6 jit_solution(14033231231247904284)
XLA Ops:
  1.9 126.2 %shard_map.111 = (bf16[128,1152]{1,0:T(8,128)(2,1)}, bf16[128,1152]{1,0:T(8,128)(2,1)}, f32[36,1152]{1,0:T(8,128)}, f32[36,1152]{1,0:T(8,128)}) custom-call(bf16[128,1152]{1,0:T(8,128)(2,1)} %ximg.1, bf16[128,1152]{1,0:T(8,128)(2,1)} %xtxt.1, bf16[36,1152]{1,0:T(8,128)(2,1)} %wimg.1, bf16[36,1152]{1,0:T(8,128)(2,1)} %wtxt.1, s32[1,128]{1,0:T(1,128)} %bitcast.2, ...), custom_call_target="tpu_custom_call" | custom-call | flops 6000000000 | bytes 4000000 | tf_op jit(solution)/shard_map/pallas_call | solution.py:528
  128.2 0.0 copy-start
  128.2 1.7 %copy.18 = bf16[128,1152]{1,0:T(8,128)(2,1)} copy(bf16[128,1152]{1,0:T(8,128)(2,1)} %get-tuple-element.8) | data formatting | bytes 589824
  129.9 0.0 copy-done
  129.9 0.0 copy-start.2
  129.9 0.7 copy.19
  130.6 0.3 copy-done.2
  130.9 0.0 copy-start.1
  130.9 0.7 copy.20
  131.6 0.3 copy-done.1
  131.9 0.7 copy.21
Async XLA Ops:
  128.2 1.8 %copy-start = (bf16[128,1152]{1,0:T(8,128)(2,1)S(1)}, bf16[128,1152]{1,0:T(8,128)(2,1)}, u32[]{:S(2)}) copy-start(bf16[128,1152]{1,0:T(8,128)(2,1)} %get-tuple-element.9) | copy-start | bytes 884740
  129.9 1.0 copy-start.2
  130.9 1.0 copy-start.1

commit v5 on v3

--- a/solution.py
+++ b/solution.py
@@ -96,9 +96,9 @@
         slot = wbuf.at[w, 2 * zat(k) + c, pick(k, across[1], across[2])]
         return copy(slot, slot, wx_s.at[w, k, 3], wx_r.at[w, k, 3], (dp, pick(k, across[2], across[1])))
 
-    def w_c(w, k, j):
-        slot = wbuf.at[w, 2 * zat(k) + c, whose(j)]
-        return copy(slot, slot, wc_s.at[w, k, j], wc_r.at[w, k, j], core)
+    def w_c(w, k):
+        slot = wbuf.at[w, 2 * zat(k) + c]
+        return copy(slot, slot, wc_s.at[w, k], wc_r.at[w, k], core)
 
     def w_z_wait(w, k):
         slot = wbuf.at[w, 2 * zat(k) + c, m]
@@ -108,9 +108,9 @@
         slot = wbuf.at[w, 2 * zat(k) + c, whose(j)]
         copy(slot, slot, wx_s.at[w, k, j], wx_r.at[w, k, j], core).wait_recv()
 
-    def w_c_wait(w, k, j):
-        slot = wbuf.at[w, 2 * zat(k) + other, whose(j)]
-        copy(slot, slot, wc_s.at[w, k, j], wc_r.at[w, k, j], core).wait_recv()
+    def w_c_wait(w, k):
+        slot = wbuf.at[w, 2 * zat(k) + other]
+        copy(slot, slot, wc_s.at[w, k], wc_r.at[w, k], core).wait_recv()
 
     def w_start(w):
         for k in range(1, nz):
@@ -118,14 +118,12 @@
         wbuf[w, dp, m] = w_refs[w][...]
         for j in near:
             w_x(w, 0, j).start()
-        w_c(w, 0, 0).start()
 
     def w_pass_z(w):
         def body(k):
             w_z_wait(w, k)
             for j in near:
                 w_x(w, k, j).start()
-            w_c(w, k, 0).start()
 
         loop(1, nz, body)
 
@@ -133,7 +131,6 @@
         def body(k):
             for j in near:
                 w_x_wait(w, k, j)
-                w_c(w, k, j).start()
             if square:
                 w_diag(w, k).start()
 
@@ -148,15 +145,14 @@
         def own(k):
             if square:
                 w_x_wait(w, k, 3)
-                w_c(w, k, 3).start()
+            w_c(w, k).start()
             if group == 1:
                 join(w, 2 * zat(k) + c)
 
         loop(0, nz, own)
 
         def rest(k):
-            for j in range(nm):
-                w_c_wait(w, k, j)
+            w_c_wait(w, k)
             if group == 1:
                 join(w, 2 * zat(k) + other)
 
@@ -274,20 +270,23 @@
         slope = (-sign * jax.nn.sigmoid(-sign * logits)).astype(BF16)
         slopes[:, span] = slope
         part = dot(slope, imgs[...], 0, 0)
+        turn = lax.rem(k, 2)
         for h in range(2):
-            dt[h] = part[h * rows:(h + 1) * rows, :]
-        tcs[k] = dt[other].astype(BF16)
+            @pl.when(c == h)
+            def _():
+                dt[turn] = part[h * rows:(h + 1) * rows, :]
+                tcs[k] = part[(1 - h) * rows:(2 - h) * rows, :].astype(BF16)
+
         grad_core(k).start()
+
+        @pl.when(i > 1)
+        def _():
+            sum_core(i - 1)
+
+    def sum_core(k):
         grad_core(k).wait_recv()
-
-        @pl.when(k > 0)
-        def _():
-            tzs[k] = (dt[c] + tcr[k].astype(F32)).astype(BF16)
-            grad_z(k).start()
-
-        @pl.when(k == 0)
-        def _():
-            gown[TXT] = dt[c] + tcr[k].astype(F32)
+        tzs[k] = (dt[lax.rem(k, 2)] + tcr[k].astype(F32)).astype(BF16)
+        grad_z(k).start()
 
     loop(1, nz + 1, pair)
 
@@ -307,6 +306,8 @@
             gown[IMG] = part
 
     loop(1, nm + 1, img_part)
+    grad_core(0).wait_recv()
+    gown[TXT] = dt[0] + tcr[0].astype(F32)
 
     def rs_core(w, k):
         return copy(rcs.at[w, k], rcr.at[w, k], rc_s.at[w, k], rc_r.at[w, k], core)
@@ -402,18 +403,18 @@
         grad_img(j).wait_recv()
         grad = grad + dir_[j].astype(F32)
     backward(IMG, sim * grad)
-    gimg[...] = dot(dpre[IMG], wfull[IMG], 1, 1).astype(BF16)
-    to_mp(IMG)
-    to_y(IMG)
     grad = gown[TXT]
     for k in range(1, nz):
         grad_z(k).wait_recv()
         grad = grad + tzr[k].astype(F32)
     backward(TXT, sim * grad)
+    to_mp(IMG)
     to_mp(TXT)
-    to_z(IMG)
+    gimg[...] = dot(dpre[IMG], wfull[IMG], 1, 1).astype(BF16)
+    to_y(IMG)
     to_y(TXT)
     gtxt[...] = dot(dpre[TXT], wfull[TXT], 1, 1).astype(BF16)
+    to_z(IMG)
     to_z(TXT)
     finish(IMG, dwimg)
     finish(TXT, dwtxt)
@@ -432,8 +433,7 @@
         grad_img(j).wait_send()
     for w in (TXT, IMG):
         def body(k):
-            for j in range(nm):
-                w_c(w, k, j).wait_send()
+            w_c(w, k).wait_send()
             rs_core(w, k).wait_send()
             for j in near:
                 w_x(w, k, j).wait_send()
@@ -462,7 +462,7 @@
     dma = pltpu.SemaphoreType.DMA
     vm = pltpu.VMEM
     sems = [
-        dma((2, nz)), dma((2, nz)), dma((2, nz, nm)), dma((2, nz, nm)), dma((2, nz, nm)), dma((2, nz, nm)),
+        dma((2, nz)), dma((2, nz)), dma((2, nz, nm)), dma((2, nz, nm)), dma((2, nz)), dma((2, nz)),
         dma((nm,)), dma((nm,)), dma((nz,)), dma((nz,)), dma((nz,)), dma((nz,)),
         dma((nm,)), dma((nm,)), dma((nz,)), dma((nz,)), dma((nz,)), dma((nz,)),
         dma((nz,)), dma((nz,)), dma((nz,)), dma((nz,)), dma((nm,)), dma((nm,)),
@@ -493,8 +493,8 @@
         vm((2, nz, big, width), BF16),
         vm((2, nz, nm, wrows, width), BF16),
         vm((2, nz, 2 if nm == 4 else nm, wrows, width), BF16),
-        vm((2, nz, wrows, width), BF16),
-        vm((2, nz, wrows, width), BF16),
+        vm((2, nz if nm == 4 else 1, wrows, width), BF16),
+        vm((2, nz if nm == 4 else 1, wrows, width), BF16),
         vm((2, nz, wrows, width), BF16),
         vm((2, nz, wrows, width), BF16),
         vm((2, wrows, width), F32),
@@ -513,7 +513,7 @@
         out_specs=(whole,) * 4,
         scratch_shapes=scratch + sems,
         compiler_params=pltpu.CompilerParams(
-            collective_id=0, has_side_effects=True, vmem_limit_bytes=62 * 1024 * 1024
+            collective_id=0, has_side_effects=True, vmem_limit_bytes=63 * 1024 * 1024
         ),
         cost_estimate=pl.CostEstimate(flops=6 * 10**9, bytes_accessed=4 * 10**6, transcendentals=0),
     )(

time: 130 us -> 130 us (level)
  no operation moved by 1% of the time
where the time goes in v5:
time: 130 us
  Pallas kernels  123 us (95%)
  local copies, waits for them, and re-layouts  4.44 us (3%)
  between operations  1.94 us (1%)
    pallas_call x1, Pallas kernels, call(): pl.pallas_call(functools.partial(kernel, nz, nm, rows, wrows), out_shape=...  123 us
    unnamed x10, local copies, waits for them, and re-layouts  4.44 us

profile of v5, /device:TPU:0, one launch (start us, length us, event | category | flops | bytes accessed | tf_op | source)
XLA Modules:
  0.0 129.8 jit_solution(11109487499503057031)
XLA Ops:
  1.9 123.4 %shard_map.111 = (bf16[128,1152]{1,0:T(8,128)(2,1)}, bf16[128,1152]{1,0:T(8,128)(2,1)}, f32[36,1152]{1,0:T(8,128)}, f32[36,1152]{1,0:T(8,128)}) custom-call(bf16[128,1152]{1,0:T(8,128)(2,1)} %ximg.1, bf16[128,1152]{1,0:T(8,128)(2,1)} %xtxt.1, bf16[36,1152]{1,0:T(8,128)(2,1)} %wimg.1, bf16[36,1152]{1,0:T(8,128)(2,1)} %wtxt.1, s32[1,128]{1,0:T(1,128)} %bitcast.2, ...), custom_call_target="tpu_custom_call" | custom-call | flops 6000000000 | bytes 4000000 | tf_op jit(solution)/shard_map/pallas_call | solution.py:504
  125.4 0.0 copy-start
  125.4 1.7 %copy.18 = bf16[128,1152]{1,0:T(8,128)(2,1)} copy(bf16[128,1152]{1,0:T(8,128)(2,1)} %get-tuple-element.8) | data formatting | bytes 589824
  127.1 0.0 copy-done
  127.1 0.0 copy-start.2
  127.1 0.7 copy.19
  127.8 0.3 copy-done.2
  128.2 0.0 copy-start.1
  128.2 0.7 copy.20
  128.8 0.3 copy-done.1
  129.1 0.7 copy.21
Async XLA Ops:
  125.4 1.8 %copy-start = (bf16[128,1152]{1,0:T(8,128)(2,1)S(1)}, bf16[128,1152]{1,0:T(8,128)(2,1)}, u32[]{:S(2)}) copy-start(bf16[128,1152]{1,0:T(8,128)(2,1)} %get-tuple-element.9) | copy-start | bytes 884740
  127.1 1.0 copy-start.2
  128.2 1.0 copy-start.1
